TPU v7x, 32 devices: a whole 2x2x4 slice. The times are simulated.
32 devices in a mesh: sample: 4 (over y, x), feat: 8 (over z, core).
Axes of the slice: x: 2, y: 2, z: 4, core: 2. Of those that a mesh axis runs over, the one named last changes fastest.
Arguments:
- view_a: bfloat16 [512, 16384], P('sample', 'feat'), may hold values from -60 to 60
- view_b: bfloat16 [512, 16384], P('sample', 'feat'), may hold values from -60 to 60
Outputs:
- loss: float32 [], replicated
- grad_a: bfloat16 [512, 16384], P('sample', 'feat')
- grad_b: bfloat16 [512, 16384], P('sample', 'feat')
All inputs are finite; a program needn't handle non-finite values.
Results may differ from a plain program's by a relative error of at most 0.02.
Values may be sent and summed in bfloat16 or wider, within the bound.
A program may use at most 128 MiB of HBM per device.

v0:
```python
import jax
import jax.numpy as jnp
from jax import lax
from jax.sharding import PartitionSpec as P

EPSILON = 1e-05
OFF_WEIGHT = 0.0051


def body(view_a, view_b):
    rows_dev, cols_dev = view_a.shape
    groups = lax.axis_size("sample")
    blocks = lax.axis_size("feat")
    total_rows = rows_dev * groups
    sub_width = cols_dev // groups
    inv_rows = 1.0 / total_rows
    sample_id = lax.axis_index("sample")
    feat_id = lax.axis_index("feat")
    float_a = view_a.astype(jnp.float32)
    float_b = view_b.astype(jnp.float32)
    moment_sums = lax.psum(
        (
            jnp.sum(float_a, axis=0),
            jnp.sum(float_a * float_a, axis=0),
            jnp.sum(float_b, axis=0),
            jnp.sum(float_b * float_b, axis=0),
        ),
        "sample",
    )
    mean_a = moment_sums[0] * inv_rows
    scale_a = lax.rsqrt(moment_sums[1] * inv_rows - mean_a * mean_a + EPSILON)
    mean_b = moment_sums[2] * inv_rows
    scale_block_b = lax.rsqrt(moment_sums[3] * inv_rows - mean_b * mean_b + EPSILON)
    local_a = ((float_a - mean_a) * scale_a).astype(jnp.bfloat16)
    source_b = ((float_b - mean_b) * scale_block_b).astype(jnp.bfloat16)
    scale_b = lax.dynamic_slice_in_dim(scale_block_b, sample_id * sub_width, sub_width)
    norm_a = lax.all_gather(local_a, "sample", axis=0, tiled=True)
    row_index = jnp.arange(cols_dev, dtype=jnp.int32)
    wide_b = lax.all_gather(source_b, "feat", axis=1, tiled=True)
    arranged = (
        wide_b.reshape(rows_dev, blocks, groups, sub_width)
        .transpose(0, 2, 1, 3)
        .reshape(rows_dev, blocks * cols_dev)
    )
    moved_b = lax.all_to_all(arranged, "sample", split_axis=1, concat_axis=0, tiled=True)
    own_b = lax.dynamic_slice_in_dim(moved_b, feat_id * sub_width, sub_width, 1)
    panel_width = moved_b.shape[1]
    correlation = (
        lax.dot_general(
            norm_a, moved_b, (((0,), (0,)), ((), ())), preferred_element_type=jnp.float32
        )
        * inv_rows
    )
    local_cols = jnp.arange(panel_width, dtype=jnp.int32)
    owner_block = local_cols // sub_width
    offset = local_cols % sub_width
    on_diagonal = (owner_block[None, :] == feat_id) & (
        offset[None, :] + sample_id * sub_width == row_index[:, None]
    )
    missing = 1.0 - correlation
    piece_loss = jnp.sum(
        jnp.where(on_diagonal, missing * missing, OFF_WEIGHT * correlation * correlation)
    )
    factor = jnp.where(on_diagonal, correlation - 1.0, OFF_WEIGHT * correlation).astype(
        jnp.bfloat16
    )
    grad_rows = lax.dot_general(
        moved_b, factor, (((1,), (1,)), ((), ())), preferred_element_type=jnp.float32
    )
    folded = (piece_loss, grad_rows, factor)
    loss_sum, grad_rows, factor_tile = folded
    row_grad = lax.psum_scatter(
        grad_rows.astype(jnp.bfloat16), "sample", scatter_dimension=0, tiled=True
    ).astype(jnp.float32)
    float_local = local_a.astype(jnp.float32)
    moments = lax.psum(
        (jnp.sum(row_grad, axis=0), jnp.sum(row_grad * float_local, axis=0)), "sample"
    )
    grad_a = (
        scale_a * (row_grad - moments[0] * inv_rows - float_local * (moments[1] * inv_rows))
    ).astype(jnp.bfloat16)
    col_grad = lax.psum_scatter(
        lax.dot_general(
            factor_tile, norm_a, (((0,), (1,)), ((), ())), preferred_element_type=jnp.float32
        ).astype(jnp.bfloat16),
        "feat",
        scatter_dimension=0,
        tiled=True,
    ).astype(jnp.float32)
    own_t = own_b.T.astype(jnp.float32)
    mean_grad = jnp.mean(col_grad, axis=1, keepdims=True)
    mean_cross = jnp.mean(col_grad * own_t, axis=1, keepdims=True)
    grad_b_t = (scale_b[:, None] * (col_grad - mean_grad - own_t * mean_cross)).astype(jnp.bfloat16)
    returned = lax.all_to_all(grad_b_t, "sample", split_axis=1, concat_axis=0, tiled=True)
    grad_b = returned.T
    loss = lax.psum(loss_sum, ("sample", "feat")) / (cols_dev * blocks)
    return (loss, grad_a, grad_b)


def solution(mesh):
    in_specs = (P("sample", "feat"), P("sample", "feat"))
    out_specs = (P(), P("sample", "feat"), P("sample", "feat"))
    return jax.shard_map(body, mesh=mesh, in_specs=in_specs, out_specs=out_specs, check_vma=False)
```

profile of v0, /device:TPU:0, one launch (start us, length us, event | category | flops | bytes accessed | tf_op | source)
XLA Modules:
  0.0 308.1 jit_solution(12647547749197257244)
XLA Ops:
  7.2 1.5 convert_reduce_fusion.2
  8.7 17.8 %all-reduce.1 = (f32[2048]{0:T(1024)S(1)}, f32[2048]{0:T(1024)S(1)}, f32[2048]{0:T(1024)S(1)}, f32[2048]{0:T(1024)S(1)}) all-reduce(f32[2048]{0:T(1024)S(1)} %get-tuple-element.23, f32[2048]{0:T(1024)S(1)} %get-tuple-element.24, f32[2048]{0:T(1024)S(1)} %get-tuple-element.8, ...), channel_id=1, replica_groups=mesh['sample'=4,'feat'=8] {'sample'}, use_global_device_ids=true, to_apply=%region_3.0 | all-reduce | flops 8192 | bytes 65536 | tf_op jit(solution)/shard_map/psum | solution.py:21
  26.5 2.0 fusion.8
  28.6 2.0 fusion.5
  30.6 44.6 %all-gather.5.cloned.1.call-done = bf16[128,16384]{1,0:T(8,128)(2,1)} async-done(((bf16[128,2048]{1,0:T(8,128)(2,1)}), bf16[128,16384]{1,0:T(8,128)(2,1)}) %all-gather.5.cloned.1.call-update) | async-done | bytes 4194320 | tf_op jit(solution)/shard_map/all_gather | solution.py:39
  75.2 7.8 %reshape.58 = bf16[128,8,4,512]{3,2,1,0:T(4,128)(2,1)} reshape(bf16[128,16384]{1,0:T(8,128)(2,1)} %all-gather.5.cloned.1.call-done) | data formatting | bytes 8388608 | tf_op jit(solution)/shard_map/reshape | solution.py:41
  83.0 7.9 %copy.7 = bf16[128,8,4,512]{0,3,1,2:T(8,128)(2,1)} copy(bf16[128,8,4,512]{3,2,1,0:T(4,128)(2,1)} %reshape.58) | data formatting | bytes 8388608 | tf_op jit(solution)/shard_map/reshape | solution.py:41
  90.9 4.9 %all-to-all-start = ((bf16[128,4,4096]{0,2,1:T(8,128)(2,1)}), bf16[128,4,4096]{0,2,1:T(8,128)(2,1)}, u32[]{:S(2)}, u32[]{:S(2)}) async-start(bf16[128,4,4096]{0,2,1:T(8,128)(2,1)} %bitcast.38), calls=%async_computation | async-start | bytes 8388608 | tf_op jit(solution)/shard_map/all_to_all | solution.py:45
  95.9 49.2 %all-gather.3.cloned.1.call-done = bf16[512,2048]{1,0:T(8,128)(2,1)} async-done(((bf16[128,2048]{1,0:T(8,128)(2,1)}), bf16[512,2048]{1,0:T(8,128)(2,1)}) %all-gather.3.cloned.1.call-update) | async-done | bytes 2097168 | tf_op jit(solution)/shard_map/all_gather | solution.py:37
  145.1 10.1 %all-to-all-done = bf16[128,4,4096]{0,2,1:T(8,128)(2,1)} async-done(((bf16[128,4,4096]{0,2,1:T(8,128)(2,1)}), bf16[128,4,4096]{0,2,1:T(8,128)(2,1)}, u32[]{:S(2)}, u32[]{:S(2)}) %all-to-all-start) | async-done | bytes 4194336 | tf_op jit(solution)/shard_map/all_to_all | solution.py:45
  155.1 25.7 %select_reduce_fusion = (f32[]{:T(128)}, f32[2048,4096]{1,0:T(8,128)}) fusion(s32[4096]{0:T(1024)S(1)} %fusion.23, pred[4096]{0:T(1024)(128)(4,1)S(1)} %fusion.22, bf16[512,2048]{1,0:T(8,128)(2,1)} %all-gather.3.cloned.1.call-done, bf16[128,4,4096]{0,2,1:T(8,128)(2,1)} %all-to-all-done), kind=kOutput, calls=%fused_computation.1 | convolution fusion | flops 8665432064 | bytes 39866372 | tf_op jit(solution)/shard_map/dot_general | solution.py:49
  180.9 18.1 %convolution_convert_fusion.1 = bf16[512,2048]{1,0:T(8,128)(2,1)} fusion(f32[2048,4096]{1,0:T(8,128)} %get-tuple-element.22, s32[4096]{0:T(1024)S(1)} %fusion.23, pred[4096]{0:T(1024)(128)(4,1)S(1)} %fusion.22, bf16[128,4,4096]{0,2,1:T(8,128)(2,1)} %all-to-all-done), kind=kOutput, calls=%fused_computation.6 | convolution fusion | flops 8649703424 | bytes 39866368 | tf_op jit(solution)/shard_map/dot_general | solution.py:67
  199.1 22.1 %convolution_convert_fusion = bf16[4096,512]{1,0:T(8,128)(2,1)} fusion(bf16[512,2048]{1,0:T(8,128)(2,1)S(1)} %copy-done.1, f32[2048,4096]{1,0:T(8,128)} %get-tuple-element.22, s32[4096]{0:T(1024)S(1)} %fusion.23, pred[4096]{0:T(1024)(128)(4,1)S(1)} %fusion.22), kind=kOutput, calls=%fused_computation.4 | convolution fusion | flops 8650752000 | bytes 39866368 | tf_op jit(solution)/shard_map/dot_general | solution.py:83
  221.2 38.6 %psum.53 = f32[]{:T(128)} all-reduce(f32[]{:T(128)} %get-tuple-element.21), channel_id=1, replica_groups=mesh['sample'=4,'feat'=8] {'sample','feat'}, use_global_device_ids=true, to_apply=%region_9.10 | all-reduce | flops 1 | bytes 8 | tf_op jit(solution)/shard_map/psum | solution.py:96
  260.4 4.6 %copy_bitcast_fusion = bf16[512,4096]{0,1:T(8,128)(2,1)} fusion(bf16[128,4,4096]{0,2,1:T(8,128)(2,1)} %all-to-all-done), kind=kLoop, calls=%fused_computation.5 | loop fusion | bytes 8388608 | tf_op jit(solution)/shard_map/all_to_all | solution.py:45
  265.1 1.3 convert_reduce_fusion.1
  266.4 17.0 %all-reduce = (f32[2048]{0:T(1024)S(1)}, f32[2048]{0:T(1024)S(1)}) all-reduce(f32[2048]{0:T(1024)S(1)} %get-tuple-element.6, f32[2048]{0:T(1024)S(1)} %get-tuple-element.5), channel_id=1, replica_groups=mesh['sample'=4,'feat'=8] {'sample'}, use_global_device_ids=true, to_apply=%region_14.15 | all-reduce | flops 4096 | bytes 32768 | tf_op jit(solution)/shard_map/psum | solution.py:76
  283.4 1.8 reduce-scatter.5.cloned.1.call-done
  285.2 1.5 convert_reduce_fusion
  286.7 2.4 copy_bitcast_fusion.1
  289.1 3.7 %all-to-all-start.1 = ((bf16[512,4,128]{2,0,1:T(8,128)(2,1)}), bf16[512,4,128]{2,0,1:T(8,128)(2,1)S(1)}, u32[]{:S(2)}, u32[]{:S(2)}) async-start(bf16[512,4,128]{2,0,1:T(8,128)(2,1)} %copy_bitcast_fusion.1), calls=%async_computation.3 | async-start | bytes 1048576 | tf_op jit(solution)/shard_map/all_to_all | solution.py:94
  292.8 2.1 fusion.3
  294.9 4.5 %all-to-all-done.1 = bf16[512,4,128]{2,0,1:T(8,128)(2,1)S(1)} async-done(((bf16[512,4,128]{2,0,1:T(8,128)(2,1)}), bf16[512,4,128]{2,0,1:T(8,128)(2,1)S(1)}, u32[]{:S(2)}, u32[]{:S(2)}) %all-to-all-start.1) | async-done | bytes 524320 | tf_op jit(solution)/shard_map/all_to_all | solution.py:94
  299.4 1.0 copy.10
  (22 shorter events, 0.4 us)
Async XLA Ops:
  7.2 68.0 %all-gather.5.cloned.1.call-start = ((), (), s32[]{:S(2)}) async-start(), calls=%async_computation.5 | async-start | bytes 4718592 | tf_op jit(solution)/shard_map/all_gather | solution.py:39
  28.5 116.6 %all-gather.3.cloned.1.call-start = ((), (), s32[]{:S(2)}) async-start(), calls=%async_computation.4 | async-start | bytes 2621440 | tf_op jit(solution)/shard_map/all_gather | solution.py:37
  90.9 64.2 %all-to-all-start = ((bf16[128,4,4096]{0,2,1:T(8,128)(2,1)}), bf16[128,4,4096]{0,2,1:T(8,128)(2,1)}, u32[]{:S(2)}, u32[]{:S(2)}) async-start(bf16[128,4,4096]{0,2,1:T(8,128)(2,1)} %bitcast.38), calls=%async_computation | async-start | bytes 8388608 | tf_op jit(solution)/shard_map/all_to_all | solution.py:45
  95.8 169.3 %reduce-scatter.3.cloned.1.call-start = ((), (), s32[]{:S(2)}) async-start(), calls=%async_computation.6 | async-start | bytes 2621440 | tf_op jit(solution)/shard_map/reduce_scatter | solution.py:72
  180.9 18.2 %copy-start.1 = (bf16[512,2048]{1,0:T(8,128)(2,1)S(1)}, bf16[512,2048]{1,0:T(8,128)(2,1)}, u32[]{:S(2)}) copy-start(bf16[512,2048]{1,0:T(8,128)(2,1)} %all-gather.3.cloned.1.call-done) | copy-start | bytes 6291460
  199.0 86.2 %reduce-scatter.5.cloned.1.call-start = ((), (), s32[]{:S(2)}) async-start(), calls=%async_computation.7 | async-start | bytes 4718592 | tf_op jit(solution)/shard_map/reduce_scatter | solution.py:82
  221.1 44.0 %copy-start = (bf16[128,2048]{1,0:T(8,128)(2,1)S(1)}, bf16[128,2048]{1,0:T(8,128)(2,1)}, u32[]{:S(2)}) copy-start(bf16[128,2048]{1,0:T(8,128)(2,1)} %param.2) | copy-start | bytes 1572868
  289.1 10.2 %all-to-all-start.1 = ((bf16[512,4,128]{2,0,1:T(8,128)(2,1)}), bf16[512,4,128]{2,0,1:T(8,128)(2,1)S(1)}, u32[]{:S(2)}, u32[]{:S(2)}) async-start(bf16[512,4,128]{2,0,1:T(8,128)(2,1)} %copy_bitcast_fusion.1), calls=%async_computation.3 | async-start | bytes 1048576 | tf_op jit(solution)/shard_map/all_to_all | solution.py:94
Sparse Core Ops, SparseCore 0:
  28.6 46.5 all-gather.4
  77.6 67.3 all-gather.2
  199.1 33.5 reduce-scatter.2
  235.0 50.1 reduce-scatter.4
where the time goes:
time: 309 us; the launch traced here: 308 us
  waiting for transfers between devices  110 us (36%)
  blocking collectives  73.3 us (24%)
  matrix products  65.9 us (21%)
  local copies, waits for them, and re-layouts  21.4 us (7%)
  between operations  15.6 us (5%)
  other arithmetic  12.9 us (4%)
  starting transfers between devices  8.68 us (3%)
    all_gather x1, waiting for transfers between devices, body(): norm_a = lax.all_gather(local_a, 'sample', axis=0, tiled=True)  49.2 us
    all_gather x1, waiting for transfers between devices, body(): wide_b = lax.all_gather(source_b, 'feat', axis=1, tiled=True)  44.6 us
    psum x1, blocking collectives, body(): loss = lax.psum(loss_sum, ('sample', 'feat')) / (cols_dev * blocks)  38.6 us
    dot_general x1, matrix products, body(): lax.dot_general(norm_a, moved_b, (((0,), (0,)), ((), ())), preferred_elem...  25.7 us
    dot_general x1, matrix products, body(): lax.dot_general(factor_tile, norm_a, (((0,), (1,)), ((), ())), preferred_...  22.1 us
    dot_general x1, matrix products, body(): lax.dot_general(moved_b, factor, (((1,), (1,)), ((), ())), preferred_elem...  18.1 us
    psum x1, blocking collectives, body(): lax.psum((jnp.sum(float_a, axis=0), jnp.sum(float_a * float_a, axis=0), j...  17.8 us
    psum x1, blocking collectives, body(): lax.psum((jnp.sum(row_grad, axis=0), jnp.sum(row_grad * float_local, axis...  17 us
  transfers between devices with their start and end apart: 6, of which 5 were waited for; matrix products, arithmetic and copies ran while one was open for 16% of the time, Pallas kernels for 0%

commit v1 on v0

v1 whole, which is shorter than its diff:
```python
import jax
import jax.numpy as jnp
from jax import lax
from jax.sharding import PartitionSpec as P

EPSILON = 1e-05
OFF_WEIGHT = 0.0051


def gram(x):
    return lax.dot_general(x, x, (((1,), (1,)), ((), ())), preferred_element_type=jnp.float32)


def apply_gram(g, x):
    high = g.astype(jnp.bfloat16)
    low = (g - high.astype(jnp.float32)).astype(jnp.bfloat16)
    dims = (((1,), (0,)), ((), ()))
    return lax.dot_general(
        high, x, dims, preferred_element_type=jnp.float32
    ) + lax.dot_general(low, x, dims, preferred_element_type=jnp.float32)


def normalize(raw, inv_rows):
    floats = raw.astype(jnp.float32)
    mean = jnp.sum(floats, axis=0) * inv_rows
    scale = lax.rsqrt(jnp.sum(floats * floats, axis=0) * inv_rows - mean * mean + EPSILON)
    return ((floats - mean) * scale).astype(jnp.bfloat16), scale


def backnorm(grad, normed, scale, inv_rows):
    floats = normed.astype(jnp.float32)
    mean_grad = jnp.sum(grad, axis=0) * inv_rows
    mean_cross = jnp.sum(grad * floats, axis=0) * inv_rows
    return (scale * (grad - mean_grad - floats * mean_cross)).astype(jnp.bfloat16)


def body(view_a, view_b):
    rows_dev, cols_dev = view_a.shape
    groups = lax.axis_size("sample")
    blocks = lax.axis_size("feat")
    total_rows = rows_dev * groups
    features = cols_dev * blocks
    inv_rows = 1.0 / total_rows
    views = lax.all_to_all(
        jnp.stack((view_a, view_b)), "sample", split_axis=2, concat_axis=1, tiled=True
    )
    norm_a, scale_a = normalize(views[0], inv_rows)
    norm_b, scale_b = normalize(views[1], inv_rows)
    diag = jnp.sum(norm_a.astype(jnp.float32) * norm_b.astype(jnp.float32), axis=0) * inv_rows
    diag_loss = jnp.sum((1.0 - diag) * (1.0 - diag) - OFF_WEIGHT * diag * diag)
    grams, diag_loss = lax.psum(
        (jnp.stack((gram(norm_a), gram(norm_b))), diag_loss), ("sample", "feat")
    )
    all_loss = jnp.sum(grams[0] * grams[1]) * (OFF_WEIGHT * inv_rows * inv_rows)
    loss = (diag_loss + all_loss) / features
    extra = (1.0 - OFF_WEIGHT) * diag - 1.0
    weight = OFF_WEIGHT * inv_rows
    grad_na = weight * apply_gram(grams[1], norm_a) + extra * norm_b.astype(jnp.float32)
    grad_nb = weight * apply_gram(grams[0], norm_b) + extra * norm_a.astype(jnp.float32)
    grads = jnp.stack(
        (
            backnorm(grad_na, norm_a, scale_a, inv_rows),
            backnorm(grad_nb, norm_b, scale_b, inv_rows),
        )
    )
    grads = lax.all_to_all(grads, "sample", split_axis=1, concat_axis=2, tiled=True)
    return (loss, grads[0], grads[1])


def solution(mesh):
    in_specs = (P("sample", "feat"), P("sample", "feat"))
    out_specs = (P(), P("sample", "feat"), P("sample", "feat"))
    return jax.shard_map(body, mesh=mesh, in_specs=in_specs, out_specs=out_specs, check_vma=False)
```

time: 309 us -> 238 us (0.77)
  matrix products: 65.9 us -> 5.68 us
  waiting for transfers between devices: 110 us -> 132 us
  local copies, waits for them, and re-layouts: 21.4 us -> 9.28 us
  blocking collectives: 73.3 us -> 64.4 us
  other arithmetic: 12.9 us -> 6.38 us
  starting transfers between devices: 8.68 us -> 3.55 us
    psum x0 -> x1, waiting for transfers between devices: none -> 132 us  [body(): lax.psum((jnp.stack((gram(norm_a), gram(norm_b))), diag_loss), ('sample',...]
    all_gather x2 -> x0, waiting for transfers between devices: 93.8 us -> none  [the longest x1 49.2 us: body(): norm_a = lax.all_gather(local_a, 'sample', axis=0, tiled=True)]
    dot_general x3 -> x6, matrix products: 65.9 us -> 5.68 us  [the longest x2 2.38 us: apply_gram(): lax.dot_general(high, x, dims, preferred_element_type=jnp.float32)]
    psum x3 -> x1, blocking collectives: 73.3 us -> 45.3 us  [body(): lax.psum((jnp.stack((gram(norm_a), gram(norm_b))), diag_loss), ('sample',...]
    all_to_all x0 -> x1, blocking collectives: none -> 19.1 us  [body(): lax.all_to_all(jnp.stack((view_a, view_b)), 'sample', split_axis=2, conca...]
    reshape x2 -> x0, local copies, waits for them, and re-layouts: 15.7 us -> none  [body(): wide_b.reshape(rows_dev, blocks, groups, sub_width).transpose(0, 2, 1, 3)]
    all_to_all x2 -> x1, waiting for transfers between devices: 14.5 us -> 0.01 us  [body(): lax.all_to_all(grads, 'sample', split_axis=1, concat_axis=2, tiled=True)]
    convert_element_type x3 -> x1, other arithmetic: 6.07 us -> 0.92 us  [normalize(): return (((floats - mean) * scale).astype(jnp.bfloat16), scale)]
  transfers between devices with their start and end apart: 6 -> 2, of which waited for: 5 -> 1; matrix products, arithmetic and copies ran while one was open for 16% -> 1% of each run, Pallas kernels for 0% -> 0%
where the time goes in v1:
time: 238 us
  waiting for transfers between devices  132 us (55%)
  blocking collectives  64.4 us (27%)
  between operations  16.6 us (7%)
  local copies, waits for them, and re-layouts  9.28 us (4%)
  other arithmetic  6.38 us (3%)
  matrix products  5.68 us (2%)
  starting transfers between devices  3.55 us (1%)
    psum x1, waiting for transfers between devices, body(): lax.psum((jnp.stack((gram(norm_a), gram(norm_b))), diag_loss), ('sample',...  132 us
    psum x1, blocking collectives, body(): lax.psum((jnp.stack((gram(norm_a), gram(norm_b))), diag_loss), ('sample',...  45.3 us
    all_to_all x1, blocking collectives, body(): lax.all_to_all(jnp.stack((view_a, view_b)), 'sample', split_axis=2, conca...  19.1 us
  transfers between devices with their start and end apart: 2, of which 1 were waited for; matrix products, arithmetic and copies ran while one was open for 1% of the time, Pallas kernels for 0%

profile of v1, /device:TPU:0, one launch (start us, length us, event | category | flops | bytes accessed | tf_op | source)
XLA Modules:
  0.0 238.0 jit_solution(7007464958755221755)
XLA Ops:
  7.2 1.3 pad_maximum_fusion.1
  8.5 0.8 copy.14
  9.3 19.1 %all_to_all.30 = bf16[2,128,2048]{1,0,2:T(2,128)(2,1)S(1)} all-to-all(bf16[2,128,2048]{1,0,2:T(2,128)(2,1)S(1)} %copy.14), channel_id=1, replica_groups=mesh['sample'=4,'feat'=8] {'sample'}, dimensions={2} | all-to-all | bytes 2097152 | tf_op jit(solution)/shard_map/all_to_all | solution.py:44
  28.4 0.8 copy.15
  29.9 0.8 copy-done.1
  30.6 0.5 convolution_bitcast_fusion
  31.1 0.5 convolution_bitcast_fusion.1
  31.6 1.5 pad_maximum_fusion
  33.1 0.6 multiply_add_fusion
  33.7 0.9 fusion.15
  34.6 132.1 %all-reduce.2.cloned.1.call-done = f32[2,512,512]{2,1,0:T(8,128)} async-done(((f32[2,512,512]{2,1,0:T(8,128)}), f32[2,512,512]{2,1,0:T(8,128)}) %all-reduce.2.cloned.1.call-update) | async-done | bytes 2097168 | tf_op jit(solution)/shard_map/psum | solution.py:51
  166.7 1.9 fusion.24
  168.8 1.8 fusion.26
  170.6 0.4 fusion.22
  171.1 0.6 fusion.27
  172.3 2.1 copy.16
  174.4 3.5 %all-to-all-start.1 = ((bf16[2,512,512]{2,0,1:T(2,128)(2,1)}), bf16[2,512,512]{2,0,1:T(2,128)(2,1)S(1)}, u32[]{:S(2)}, u32[]{:S(2)}) async-start(bf16[2,512,512]{2,0,1:T(2,128)(2,1)} %copy.16), calls=%async_computation.1 | async-start | bytes 2097152 | tf_op jit(solution)/shard_map/all_to_all | solution.py:66
  177.9 45.3 %psum.14 = f32[]{:T(128)} all-reduce(f32[]{:T(128)} %get-tuple-element.18), channel_id=1, replica_groups=mesh['sample'=4,'feat'=8] {'sample','feat'}, use_global_device_ids=true, to_apply=%region_6.0 | all-reduce | flops 1 | bytes 8 | tf_op jit(solution)/shard_map/psum | solution.py:51
  223.2 0.9 multiply_reduce_fusion
  225.4 1.5 fusion.29
  226.9 0.7 copy.17
  227.6 0.9 copy.19
  228.5 0.7 copy.18
  229.1 0.9 copy.20
  (22 shorter events, 1.5 us)
Async XLA Ops:
  7.2 159.5 %all-reduce.2.cloned.1.call-start = ((), (), s32[]{:S(2)}) async-start(), calls=%async_computation.2 | async-start | bytes 4194304 | tf_op jit(solution)/shard_map/psum | solution.py:51
  29.9 0.8 copy-start.1
  29.9 1.3 copy-start.3
  166.7 2.1 copy-start
  166.7 2.1 copy-start.4
  168.8 1.8 copy-start.2
  174.4 51.0 %all-to-all-start.1 = ((bf16[2,512,512]{2,0,1:T(2,128)(2,1)}), bf16[2,512,512]{2,0,1:T(2,128)(2,1)S(1)}, u32[]{:S(2)}, u32[]{:S(2)}) async-start(bf16[2,512,512]{2,0,1:T(2,128)(2,1)} %copy.16), calls=%async_computation.1 | async-start | bytes 2097152 | tf_op jit(solution)/shard_map/all_to_all | solution.py:66
Sparse Core Ops, SparseCore 0:
  33.2 133.4 all-reduce.1

commit v2 on v1

v2 whole, which is shorter than its diff:
```python
import functools

import jax
import jax.numpy as jnp
from jax import lax
from jax.experimental import pallas as pl
from jax.experimental.pallas import tpu as pltpu
from jax.sharding import PartitionSpec as P

EPSILON = 1e-05
OFF_WEIGHT = 0.0051
BLOCK = 128
CORES = 2
MESH = pl.DeviceIdType.MESH


def kernel(
    groups,
    blocks,
    view_a,
    view_b,
    out,
    loss_out,
    raw,
    norm,
    scales,
    extra,
    acc,
    send_core,
    recv_core,
    send_sample,
    recv_sample,
    send_depth,
    recv_depth,
    gram,
    full,
    grads,
    loss_core,
    loss_sample,
    loss_depth,
    send_sem,
    recv_sem,
    local_sem,
):
    rows_dev, cols_dev = view_a.shape
    total_rows = rows_dev * groups
    width = cols_dev // groups
    depth = blocks // CORES
    inv_rows = 1.0 / total_rows
    n_blocks = total_rows // BLOCK
    used = n_blocks * (n_blocks + 1) // 2 * BLOCK
    packed = acc.shape[0]
    rows_sample = packed // groups
    rows_depth = rows_sample // depth
    s = lax.axis_index("sample")
    f = lax.axis_index("feat")
    z = lax.div(f, CORES)
    c = lax.rem(f, CORES)
    other = 1 - c
    sample_peers = [(lax.rem(s + d, groups), f) for d in range(1, groups)]
    depth_peers = [(s, lax.rem(z + d, depth) * CORES + c) for d in range(1, depth)]
    sibling = (s, z * CORES + other)
    peers = sample_peers + depth_peers + [sibling]

    barrier = pltpu.get_barrier_semaphore()
    for peer in peers:
        pl.semaphore_signal(barrier, inc=1, device_id=peer, device_id_type=MESH)
    pl.semaphore_wait(barrier, len(peers))

    started = []

    def send(src, dst, peer):
        n = len(started)
        copy = pltpu.make_async_remote_copy(
            src_ref=src,
            dst_ref=dst,
            send_sem=send_sem.at[n],
            recv_sem=recv_sem.at[n],
            device_id=peer,
            device_id_type=MESH,
        )
        copy.start()
        started.append(copy)
        return copy

    def at(index, size):
        return pl.ds(pl.multiple_of(index * size, size), size)

    arriving = []
    for v, view in enumerate((view_a, view_b)):
        copies = [
            send(view.at[:, at(peer[0], width)], raw.at[v, at(s, rows_dev), :], peer)
            for peer in sample_peers
        ]
        own = pltpu.make_async_copy(
            view.at[:, at(s, width)], raw.at[v, at(s, rows_dev), :], local_sem.at[v]
        )
        own.start()
        arriving.append((copies, own))

    lanes = [slice(k, k + BLOCK) for k in range(0, width, BLOCK)]
    for v, (copies, own) in enumerate(arriving):
        own.wait()
        for copy in copies:
            copy.wait_recv()
        for cs in lanes:
            x = raw[v, :, cs].astype(jnp.float32)
            mean = jnp.sum(x, axis=0, keepdims=True) * inv_rows
            square = jnp.sum(x * x, axis=0, keepdims=True) * inv_rows
            scale = lax.rsqrt(square - mean * mean + EPSILON)
            scales[v, :, cs] = scale
            norm[v, :, cs] = ((x - mean) * scale).astype(jnp.bfloat16)

    def gram_rows(v, i):
        return lax.dot_general(
            norm[v, i * BLOCK : (i + 1) * BLOCK, :],
            norm[v, : (i + 1) * BLOCK, :],
            (((1,), (1,)), ((), ())),
            preferred_element_type=jnp.float32,
        )

    def spot(i, j):
        first = (i * (i + 1) // 2 + j) * BLOCK
        return slice(first, first + BLOCK)

    if packed > used:
        send_core[used:, :] = jnp.zeros((packed - used, BLOCK), jnp.bfloat16)
        acc[used:, :] = jnp.zeros((packed - used, BLOCK), jnp.float32)
    for i in range(n_blocks):
        strip = gram_rows(other, i)
        for j in range(i + 1):
            send_core[spot(i, j), :] = strip[:, j * BLOCK : (j + 1) * BLOCK].astype(jnp.bfloat16)
    to_core = send(send_core, recv_core, sibling)
    for i in range(n_blocks):
        strip = gram_rows(c, i)
        for j in range(i + 1):
            acc[spot(i, j), :] = strip[:, j * BLOCK : (j + 1) * BLOCK]
    part = jnp.zeros((1, BLOCK), jnp.float32)
    for cs in lanes:
        a = norm[0, :, cs].astype(jnp.float32)
        b = norm[1, :, cs].astype(jnp.float32)
        diag = jnp.sum(a * b, axis=0, keepdims=True) * inv_rows
        extra[:, cs] = (1.0 - OFF_WEIGHT) * diag - 1.0
        part = part + (1.0 - diag) * (1.0 - diag) - OFF_WEIGHT * diag * diag
    loss_core[c] = jnp.broadcast_to(part, (8, BLOCK))
    loss_copy = send(loss_core.at[c], loss_core.at[c], sibling)

    def fold(slots):
        total = slots[0]
        for k in range(1, slots.shape[0]):
            total = total + slots[k]
        return total

    to_core.wait_recv()
    acc[...] = acc[...] + recv_core[...].astype(jnp.float32)
    send_sample[...] = acc[...].astype(jnp.bfloat16)
    to_sample = [
        send(send_sample.at[at(peer[0], rows_sample), :], recv_sample.at[k], peer)
        for k, peer in enumerate(sample_peers)
    ]
    loss_copy.wait_recv()
    loss_sample[s] = fold(loss_core)
    loss_copies = [send(loss_sample.at[s], loss_sample.at[s], peer) for peer in sample_peers]

    mine = at(s, rows_sample)
    total = acc[mine, :]
    for k, copy in enumerate(to_sample):
        copy.wait_recv()
        total = total + recv_sample[k].astype(jnp.float32)
    acc[mine, :] = total
    send_depth[...] = total.astype(jnp.bfloat16)
    to_depth = [
        send(
            send_depth.at[at(lax.div(peer[1], CORES), rows_depth), :], recv_depth.at[k], peer
        )
        for k, peer in enumerate(depth_peers)
    ]
    for copy in loss_copies:
        copy.wait_recv()
    loss_depth[z] = fold(loss_sample)
    loss_copies = [send(loss_depth.at[z], loss_depth.at[z], peer) for peer in depth_peers]

    mine_depth = at(s * depth + z, rows_depth)
    total = acc[mine_depth, :]
    for k, copy in enumerate(to_depth):
        copy.wait_recv()
        total = total + recv_depth[k].astype(jnp.float32)
    gram[c, mine_depth, :] = total.astype(jnp.bfloat16)
    here = gram.at[c, mine_depth, :]
    for copy in [send(here, here, peer) for peer in depth_peers]:
        copy.wait_recv()
    here = gram.at[c, mine, :]
    for copy in [send(here, here, peer) for peer in sample_peers]:
        copy.wait_recv()
    from_core = send(gram.at[c], gram.at[c], sibling)

    for copy in loss_copies:
        copy.wait_recv()

    halves = [slice(k, min(k + 2 * BLOCK, width)) for k in range(0, width, 2 * BLOCK)]
    returning = []
    for v, g in ((other, c), (c, other)):
        if returning:
            from_core.wait_recv()
        for i in range(n_blocks):
            for j in range(i + 1):
                tile = gram[g, spot(i, j), :]
                full[i * BLOCK : (i + 1) * BLOCK, j * BLOCK : (j + 1) * BLOCK] = tile
                if j < i:
                    flipped = tile.astype(jnp.float32).T.astype(jnp.bfloat16)
                    full[j * BLOCK : (j + 1) * BLOCK, i * BLOCK : (i + 1) * BLOCK] = flipped
        for cs in halves:
            x = norm[v, :, cs]
            product = lax.dot_general(
                full[...], x, (((1,), (0,)), ((), ())), preferred_element_type=jnp.float32
            )
            x = x.astype(jnp.float32)
            grad = (OFF_WEIGHT * inv_rows) * product + extra[:, cs] * norm[g, :, cs].astype(
                jnp.float32
            )
            mean_grad = jnp.sum(grad, axis=0, keepdims=True) * inv_rows
            mean_cross = jnp.sum(grad * x, axis=0, keepdims=True) * inv_rows
            grads[v, :, cs] = (scales[v, :, cs] * (grad - mean_grad - x * mean_cross)).astype(
                jnp.bfloat16
            )
        copies = [
            send(grads.at[v, at(peer[0], rows_dev), :], out.at[v, :, at(s, width)], peer)
            for peer in sample_peers
        ]
        own = pltpu.make_async_copy(
            grads.at[v, at(s, rows_dev), :],
            out.at[v, :, at(s, width)],
            local_sem.at[2 + len(returning)],
        )
        own.start()
        returning.append((copies, own))

    product = jnp.zeros((BLOCK, BLOCK), jnp.float32)
    for i in range(n_blocks):
        for j in range(i + 1):
            pair = gram[0, spot(i, j), :].astype(jnp.float32) * gram[
                1, spot(i, j), :
            ].astype(jnp.float32)
            product = product + (pair if i == j else 2.0 * pair)
    trace = jnp.sum(product, axis=0, keepdims=True) * (OFF_WEIGHT * inv_rows * inv_rows)
    lane_loss = (fold(loss_depth)[0:1, :] + trace) * (1.0 / (cols_dev * blocks))
    loss_out[...] = jnp.broadcast_to(jnp.sum(lane_loss, axis=1, keepdims=True), (8, BLOCK))

    for copies, own in returning:
        own.wait()
        for copy in copies:
            copy.wait_recv()
    for copy in started:
        copy.wait_send()


def body(view_a, view_b):
    rows_dev, cols_dev = view_a.shape
    groups = lax.axis_size("sample")
    blocks = lax.axis_size("feat")
    depth = blocks // CORES
    total_rows = rows_dev * groups
    width = cols_dev // groups
    n_blocks = total_rows // BLOCK
    step = groups * depth * 16
    packed = -(-(n_blocks * (n_blocks + 1) // 2 * BLOCK) // step) * step
    rows_sample = packed // groups
    rows_depth = rows_sample // depth
    copies = 7 * (groups - 1) + 3 * (depth - 1) + 3
    bf16, f32 = jnp.bfloat16, jnp.float32
    vmem = pl.BlockSpec(memory_space=pltpu.VMEM)
    out, loss = pl.pallas_call(
        functools.partial(kernel, groups, blocks),
        out_shape=(
            jax.ShapeDtypeStruct((2, rows_dev, cols_dev), bf16),
            jax.ShapeDtypeStruct((8, BLOCK), f32),
        ),
        in_specs=[vmem, vmem],
        out_specs=(vmem, vmem),
        scratch_shapes=[
            pltpu.VMEM((2, total_rows, width), bf16),
            pltpu.VMEM((2, total_rows, width), bf16),
            pltpu.VMEM((2, 1, width), f32),
            pltpu.VMEM((1, width), f32),
            pltpu.VMEM((packed, BLOCK), f32),
            pltpu.VMEM((packed, BLOCK), bf16),
            pltpu.VMEM((packed, BLOCK), bf16),
            pltpu.VMEM((packed, BLOCK), bf16),
            pltpu.VMEM((groups - 1, rows_sample, BLOCK), bf16),
            pltpu.VMEM((rows_sample, BLOCK), bf16),
            pltpu.VMEM((depth - 1, rows_depth, BLOCK), bf16),
            pltpu.VMEM((2, packed, BLOCK), bf16),
            pltpu.VMEM((total_rows, total_rows), bf16),
            pltpu.VMEM((2, total_rows, width), bf16),
            pltpu.VMEM((CORES, 8, BLOCK), f32),
            pltpu.VMEM((groups, 8, BLOCK), f32),
            pltpu.VMEM((depth, 8, BLOCK), f32),
            pltpu.SemaphoreType.DMA((copies,)),
            pltpu.SemaphoreType.DMA((copies,)),
            pltpu.SemaphoreType.DMA((4,)),
        ],
        compiler_params=pltpu.CompilerParams(
            collective_id=0, has_side_effects=True, vmem_limit_bytes=48 * 1024 * 1024
        ),
    )(view_a, view_b)
    return (loss[0, 0], out[0], out[1])


def solution(mesh):
    in_specs = (P("sample", "feat"), P("sample", "feat"))
    out_specs = (P(), P("sample", "feat"), P("sample", "feat"))
    return jax.shard_map(body, mesh=mesh, in_specs=in_specs, out_specs=out_specs, check_vma=False)
```

time: 238 us -> 55.8 us (0.23)
  waiting for transfers between devices: 132 us -> 0 us
  blocking collectives: 64.4 us -> 0 us
  Pallas kernels: 0 us -> 51.3 us
  between operations: 16.6 us -> 0.65 us
  other arithmetic: 6.38 us -> 0 us
  matrix products: 5.68 us -> 0 us
  local copies, waits for them, and re-layouts: 9.28 us -> 3.66 us
  starting transfers between devices: 3.55 us -> 0 us
    psum x1 -> x0, waiting for transfers between devices: 132 us -> none  [body(): lax.psum((jnp.stack((gram(norm_a), gram(norm_b))), diag_loss), ('sample',...]
    pallas_call x0 -> x1, Pallas kernels: none -> 51.3 us  [body(): pl.pallas_call(functools.partial(kernel, groups, blocks), out_shape=(jax....]
    psum x1 -> x0, blocking collectives: 45.3 us -> none  [body(): lax.psum((jnp.stack((gram(norm_a), gram(norm_b))), diag_loss), ('sample',...]
    all_to_all x1 -> x0, blocking collectives: 19.1 us -> none  [body(): lax.all_to_all(jnp.stack((view_a, view_b)), 'sample', split_axis=2, conca...]
    dot_general x6 -> x0, matrix products: 5.68 us -> none  [the longest x2 2.38 us: apply_gram(): lax.dot_general(high, x, dims, preferred_element_type=jnp.float32)]
    all_to_all x1 -> x0, starting transfers between devices: 3.51 us -> none  [body(): lax.all_to_all(grads, 'sample', split_axis=1, concat_axis=2, tiled=True)]
    another operation x5 -> x0, other arithmetic: 3.34 us -> none  [the longest x1 1.47 us: body(): jnp.stack((gram(norm_a), gram(norm_b)))]
    another operation x2 -> x0, local copies, waits for them, and re-layouts: 2.86 us -> none  [the longest x1 2.07 us: body(): jnp.stack((backnorm(grad_na, norm_a, scale_a, inv_rows), backnorm(grad_nb...]
  transfers between devices with their start and end apart: 2 -> 0, of which waited for: 1 -> 0; matrix products, arithmetic and copies ran while one was open for 1% -> 0% of each run, Pallas kernels for 0% -> 0%
where the time goes in v2:
time: 55.8 us; the launch traced here: 55.6 us
  Pallas kernels  51.3 us (92%)
  local copies, waits for them, and re-layouts  3.66 us (7%)
  between operations  0.65 us (1%)
    pallas_call x1, Pallas kernels, body(): pl.pallas_call(functools.partial(kernel, groups, blocks), out_shape=(jax....  51.3 us
    unnamed x4, local copies, waits for them, and re-layouts  2.08 us

profile of v2, /device:TPU:0, one launch (start us, length us, event | category | flops | bytes accessed | tf_op | source)
XLA Modules:
  0.0 55.6 jit_solution(11576283477226065742)
XLA Ops:
  0.6 0.0 copy-start
  0.6 1.0 %copy-done = bf16[128,2048]{1,0:T(8,128)(2,1)S(1)} copy-done((bf16[128,2048]{1,0:T(8,128)(2,1)S(1)}, bf16[128,2048]{1,0:T(8,128)(2,1)}, u32[]{:S(2)}) %copy-start) | copy-done | bytes 524312
  1.7 0.0 copy-start.1
  1.7 1.0 %copy-done.1 = bf16[128,2048]{1,0:T(8,128)(2,1)S(1)} copy-done((bf16[128,2048]{1,0:T(8,128)(2,1)S(1)}, bf16[128,2048]{1,0:T(8,128)(2,1)}, u32[]{:S(2)}) %copy-start.1) | copy-done | bytes 524312
  2.7 51.3 %shard_map.49 = (bf16[2,128,2048]{2,1,0:T(8,128)(2,1)S(1)}, f32[8,128]{1,0:T(8,128)S(1)}) custom-call(bf16[128,2048]{1,0:T(8,128)(2,1)S(1)} %copy-done, bf16[128,2048]{1,0:T(8,128)(2,1)S(1)} %copy-done.1), custom_call_target="tpu_custom_call" | custom-call | tf_op jit(solution)/shard_map/pallas_call | solution.py:272
  54.0 0.5 slice.9
  54.5 1.1 %slice_bitcast_fusion = (bf16[128,2048]{1,0:T(8,128)(2,1)}, bf16[128,2048]{1,0:T(8,128)(2,1)}) fusion(bf16[2,128,2048]{2,1,0:T(8,128)(2,1)S(1)} %get-tuple-element.6), kind=kLoop, calls=%fused_computation | loop fusion | bytes 2097152 | tf_op jit(solution)/shard_map/squeeze | solution.py:306
Async XLA Ops:
  0.6 1.0 %copy-start = (bf16[128,2048]{1,0:T(8,128)(2,1)S(1)}, bf16[128,2048]{1,0:T(8,128)(2,1)}, u32[]{:S(2)}) copy-start(bf16[128,2048]{1,0:T(8,128)(2,1)} %view_a.1) | copy-start | bytes 1572868
  1.7 1.0 %copy-start.1 = (bf16[128,2048]{1,0:T(8,128)(2,1)S(1)}, bf16[128,2048]{1,0:T(8,128)(2,1)}, u32[]{:S(2)}) copy-start(bf16[128,2048]{1,0:T(8,128)(2,1)} %view_b.1) | copy-start | bytes 1572868

commit v3 on v2

v3 whole, which is shorter than its diff:
```python
import functools

import jax
import jax.numpy as jnp
from jax import lax
from jax.experimental import pallas as pl
from jax.experimental.pallas import tpu as pltpu
from jax.sharding import PartitionSpec as P

EPSILON = 1e-05
OFF_WEIGHT = 0.0051
BLOCK = 128
CORES = 2
MESH = pl.DeviceIdType.MESH


def kernel(
    groups,
    blocks,
    view_a,
    view_b,
    out_a,
    out_b,
    loss_out,
    raw,
    norm,
    scales,
    extra,
    acc,
    send_core,
    recv_core,
    send_sample,
    recv_sample,
    send_depth,
    recv_depth,
    gram,
    full,
    grads,
    loss_core,
    loss_sample,
    loss_depth,
    send_sem,
    recv_sem,
    local_sem,
):
    rows_dev, cols_dev = view_a.shape
    total_rows = rows_dev * groups
    width = cols_dev // groups
    depth = blocks // CORES
    inv_rows = 1.0 / total_rows
    n_blocks = total_rows // BLOCK
    used = n_blocks * (n_blocks + 1) // 2 * BLOCK
    packed = acc.shape[1]
    rows_core = packed // CORES
    rows_sample = rows_core // groups
    rows_depth = rows_sample // depth
    s = lax.axis_index("sample")
    f = lax.axis_index("feat")
    z = lax.div(f, CORES)
    c = lax.rem(f, CORES)
    other = 1 - c
    sample_peers = [(lax.rem(s + d, groups), f) for d in range(1, groups)]
    depth_peers = [(s, lax.rem(z + d, depth) * CORES + c) for d in range(1, depth)]
    sibling = (s, z * CORES + other)
    peers = sample_peers + depth_peers + [sibling]

    barrier = pltpu.get_barrier_semaphore()
    for peer in peers:
        pl.semaphore_signal(barrier, inc=1, device_id=peer, device_id_type=MESH)
    pl.semaphore_wait(barrier, len(peers))

    started = []

    def send(src, dst, peer):
        n = len(started)
        copy = pltpu.make_async_remote_copy(
            src_ref=src,
            dst_ref=dst,
            send_sem=send_sem.at[n],
            recv_sem=recv_sem.at[n],
            device_id=peer,
            device_id_type=MESH,
        )
        copy.start()
        started.append(copy)
        return copy

    def arrived(copies):
        for copy in copies:
            copy.wait_recv()

    def at(index, size):
        return pl.ds(pl.multiple_of(index * size, size), size)

    def send_view(v, view):
        copies = [
            send(view.at[:, at(peer[0], width)], raw.at[v, at(s, rows_dev), :], peer)
            for peer in sample_peers
        ]
        own = pltpu.make_async_copy(
            view.at[:, at(s, width)], raw.at[v, at(s, rows_dev), :], local_sem.at[v]
        )
        own.start()
        return copies, own

    lanes = [slice(k, k + BLOCK) for k in range(0, width, BLOCK)]

    def normalize(v):
        for cs in lanes:
            x = raw[v, :, cs].astype(jnp.float32)
            mean = jnp.sum(x, axis=0, keepdims=True) * inv_rows
            square = jnp.sum(x * x, axis=0, keepdims=True) * inv_rows
            scale = lax.rsqrt(square - mean * mean + EPSILON)
            scales[v, :, cs] = scale
            norm[v, :, cs] = ((x - mean) * scale).astype(jnp.bfloat16)

    def spot(i, j):
        first = (i * (i + 1) // 2 + j) * BLOCK
        return slice(first, first + BLOCK)

    def reduce_core(v):
        if packed > used:
            send_core[v, used:, :] = jnp.zeros((packed - used, BLOCK), jnp.bfloat16)
            acc[v, used:, :] = jnp.zeros((packed - used, BLOCK), jnp.float32)
        for i in range(n_blocks):
            strip = lax.dot_general(
                norm[v, i * BLOCK : (i + 1) * BLOCK, :],
                norm[v, : (i + 1) * BLOCK, :],
                (((1,), (1,)), ((), ())),
                preferred_element_type=jnp.float32,
            )
            for j in range(i + 1):
                tile = strip[:, j * BLOCK : (j + 1) * BLOCK]
                acc[v, spot(i, j), :] = tile
                send_core[v, spot(i, j), :] = tile.astype(jnp.bfloat16)
        return [send(send_core.at[v, at(other, rows_core), :], recv_core.at[v], sibling)]

    def reduce_sample(v):
        mine = at(c, rows_core)
        total = acc[v, mine, :] + recv_core[v].astype(jnp.float32)
        acc[v, mine, :] = total
        send_sample[v] = total.astype(jnp.bfloat16)
        return [
            send(send_sample.at[v, at(peer[0], rows_sample), :], recv_sample.at[v, k], peer)
            for k, peer in enumerate(sample_peers)
        ]

    def reduce_depth(v):
        mine = at(c * groups + s, rows_sample)
        total = acc[v, mine, :]
        for k in range(groups - 1):
            total = total + recv_sample[v, k].astype(jnp.float32)
        acc[v, mine, :] = total
        send_depth[v] = total.astype(jnp.bfloat16)
        return [
            send(
                send_depth.at[v, at(lax.div(peer[1], CORES), rows_depth), :],
                recv_depth.at[v, k],
                peer,
            )
            for k, peer in enumerate(depth_peers)
        ]

    def spread(v, rows, receivers):
        here = gram.at[v, rows, :]
        return [send(here, here, peer) for peer in receivers]

    def gather_depth(v):
        mine = at((c * groups + s) * depth + z, rows_depth)
        total = acc[v, mine, :]
        for k in range(depth - 1):
            total = total + recv_depth[v, k].astype(jnp.float32)
        gram[v, mine, :] = total.astype(jnp.bfloat16)
        return spread(v, mine, depth_peers)

    def gather_sample(v):
        return spread(v, at(c * groups + s, rows_sample), sample_peers)

    def gather_core(v):
        return spread(v, at(c, rows_core), [sibling])

    halves = [slice(k, min(k + 2 * BLOCK, width)) for k in range(0, width, 2 * BLOCK)]

    def return_grad(v, out):
        g = 1 - v
        for i in range(n_blocks):
            for j in range(i + 1):
                tile = gram[g, spot(i, j), :]
                full[i * BLOCK : (i + 1) * BLOCK, j * BLOCK : (j + 1) * BLOCK] = tile
                if j < i:
                    flipped = tile.astype(jnp.float32).T.astype(jnp.bfloat16)
                    full[j * BLOCK : (j + 1) * BLOCK, i * BLOCK : (i + 1) * BLOCK] = flipped
        copies = []
        for cs in halves:
            x = norm[v, :, cs]
            product = lax.dot_general(
                full[...], x, (((1,), (0,)), ((), ())), preferred_element_type=jnp.float32
            )
            x = x.astype(jnp.float32)
            grad = (OFF_WEIGHT * inv_rows) * product + extra[:, cs] * norm[g, :, cs].astype(
                jnp.float32
            )
            mean_grad = jnp.sum(grad, axis=0, keepdims=True) * inv_rows
            mean_cross = jnp.sum(grad * x, axis=0, keepdims=True) * inv_rows
            grads[v, :, cs] = (scales[v, :, cs] * (grad - mean_grad - x * mean_cross)).astype(
                jnp.bfloat16
            )
            size = cs.stop - cs.start
            there = out.at[:, pl.ds(pl.multiple_of(s * width + cs.start, BLOCK), size)]
            copies += [
                send(grads.at[v, at(peer[0], rows_dev), cs], there, peer)
                for peer in sample_peers
            ]
        own = pltpu.make_async_copy(
            grads.at[v, at(s, rows_dev), :], out.at[:, at(s, width)], local_sem.at[2 + v]
        )
        own.start()
        return copies, own

    def fold(slots):
        total = slots[0]
        for k in range(1, slots.shape[0]):
            total = total + slots[k]
        return total

    copies_a, own_a = send_view(0, view_a)
    for copy in copies_a:
        copy.wait_send()
    copies_b, own_b = send_view(1, view_b)
    own_a.wait()
    arrived(copies_a)
    normalize(0)
    step_a = reduce_core(0)
    arrived(step_a)
    step_a = reduce_sample(0)

    own_b.wait()
    arrived(copies_b)
    normalize(1)
    step_b = reduce_core(1)
    part = jnp.zeros((1, BLOCK), jnp.float32)
    for cs in lanes:
        a = norm[0, :, cs].astype(jnp.float32)
        b = norm[1, :, cs].astype(jnp.float32)
        diag = jnp.sum(a * b, axis=0, keepdims=True) * inv_rows
        extra[:, cs] = (1.0 - OFF_WEIGHT) * diag - 1.0
        part = part + (1.0 - diag) * (1.0 - diag) - OFF_WEIGHT * diag * diag
    loss_core[c] = jnp.broadcast_to(part, (8, BLOCK))
    loss_copies = [send(loss_core.at[c], loss_core.at[c], sibling)]

    arrived(step_b)
    step_b = reduce_sample(1)
    arrived(step_a)
    step_a = reduce_depth(0)
    arrived(loss_copies)
    loss_sample[s] = fold(loss_core)
    loss_copies = [send(loss_sample.at[s], loss_sample.at[s], peer) for peer in sample_peers]
    arrived(step_a)
    step_a = gather_depth(0)
    arrived(step_b)
    step_b = reduce_depth(1)
    arrived(loss_copies)
    loss_depth[z] = fold(loss_sample)
    loss_copies = [send(loss_depth.at[z], loss_depth.at[z], peer) for peer in depth_peers]
    arrived(step_a)
    step_a = gather_sample(0)
    arrived(step_b)
    step_b = gather_depth(1)
    arrived(step_a)
    step_a = gather_core(0)
    arrived(step_b)
    step_b = gather_sample(1)
    arrived(step_a)
    returning = [return_grad(1, out_b)]
    arrived(step_b)
    step_b = gather_core(1)
    arrived(step_b)
    returning.append(return_grad(0, out_a))

    arrived(loss_copies)
    product = jnp.zeros((BLOCK, BLOCK), jnp.float32)
    for i in range(n_blocks):
        for j in range(i + 1):
            pair = gram[0, spot(i, j), :].astype(jnp.float32) * gram[
                1, spot(i, j), :
            ].astype(jnp.float32)
            product = product + (pair if i == j else 2.0 * pair)
    trace = jnp.sum(product, axis=0, keepdims=True) * (OFF_WEIGHT * inv_rows * inv_rows)
    lane_loss = (fold(loss_depth)[0:1, :] + trace) * (1.0 / (cols_dev * blocks))
    loss_out[...] = jnp.sum(lane_loss, axis=1, keepdims=True)

    for copies, own in returning:
        own.wait()
        arrived(copies)
    for copy in started[len(copies_a) :]:
        copy.wait_send()


def body(view_a, view_b):
    rows_dev, cols_dev = view_a.shape
    groups = lax.axis_size("sample")
    blocks = lax.axis_size("feat")
    depth = blocks // CORES
    total_rows = rows_dev * groups
    width = cols_dev // groups
    n_blocks = total_rows // BLOCK
    step = CORES * groups * depth * 16
    packed = -(-(n_blocks * (n_blocks + 1) // 2 * BLOCK) // step) * step
    rows_core = packed // CORES
    rows_sample = rows_core // groups
    rows_depth = rows_sample // depth
    halves = -(-width // (2 * BLOCK))
    copies = (2 + 2 + 1 + 2 + 2 * halves) * (groups - 1) + 5 * (depth - 1) + 5
    bf16, f32 = jnp.bfloat16, jnp.float32
    vmem = pl.BlockSpec(memory_space=pltpu.VMEM)
    hbm = pl.BlockSpec(memory_space=pltpu.HBM)
    out_a, out_b, loss = pl.pallas_call(
        functools.partial(kernel, groups, blocks),
        out_shape=(
            jax.ShapeDtypeStruct((rows_dev, cols_dev), bf16),
            jax.ShapeDtypeStruct((rows_dev, cols_dev), bf16),
            jax.ShapeDtypeStruct((1, 1), f32),
        ),
        in_specs=[hbm, hbm],
        out_specs=(hbm, hbm, vmem),
        scratch_shapes=[
            pltpu.VMEM((2, total_rows, width), bf16),
            pltpu.VMEM((2, total_rows, width), bf16),
            pltpu.VMEM((2, 1, width), f32),
            pltpu.VMEM((1, width), f32),
            pltpu.VMEM((2, packed, BLOCK), f32),
            pltpu.VMEM((2, packed, BLOCK), bf16),
            pltpu.VMEM((2, rows_core, BLOCK), bf16),
            pltpu.VMEM((2, rows_core, BLOCK), bf16),
            pltpu.VMEM((2, groups - 1, rows_sample, BLOCK), bf16),
            pltpu.VMEM((2, rows_sample, BLOCK), bf16),
            pltpu.VMEM((2, depth - 1, rows_depth, BLOCK), bf16),
            pltpu.VMEM((2, packed, BLOCK), bf16),
            pltpu.VMEM((total_rows, total_rows), bf16),
            pltpu.VMEM((2, total_rows, width), bf16),
            pltpu.VMEM((CORES, 8, BLOCK), f32),
            pltpu.VMEM((groups, 8, BLOCK), f32),
            pltpu.VMEM((depth, 8, BLOCK), f32),
            pltpu.SemaphoreType.DMA((copies,)),
            pltpu.SemaphoreType.DMA((copies,)),
            pltpu.SemaphoreType.DMA((4,)),
        ],
        compiler_params=pltpu.CompilerParams(
            collective_id=0, has_side_effects=True, vmem_limit_bytes=62 * 1024 * 1024
        ),
    )(view_a, view_b)
    return (loss[0, 0], out_a, out_b)


def solution(mesh):
    in_specs = (P("sample", "feat"), P("sample", "feat"))
    out_specs = (P(), P("sample", "feat"), P("sample", "feat"))
    return jax.shard_map(body, mesh=mesh, in_specs=in_specs, out_specs=out_specs, check_vma=False)
```

time: 55.8 us -> 55.2 us (0.989)
  between operations: 0.65 us -> 2.41 us
  Pallas kernels: 51.3 us -> 49.9 us
  local copies, waits for them, and re-layouts: 3.66 us -> 2.74 us
    pallas_call x1, Pallas kernels: 51.3 us -> 49.9 us  [body(): pl.pallas_call(functools.partial(kernel, groups, blocks), out_shape=(jax....]
    squeeze x1 -> x0, local copies, waits for them, and re-layouts: 1.07 us -> none  [body(): return (loss[0, 0], out[0], out[1])]
    unnamed x4, local copies, waits for them, and re-layouts: 2.08 us -> 2.74 us
where the time goes in v3:
time: 55.2 us; the launch traced here: 55.1 us
  Pallas kernels  49.9 us (90%)
  local copies, waits for them, and re-layouts  2.74 us (5%)
  between operations  2.41 us (4%)
    pallas_call x1, Pallas kernels, body(): pl.pallas_call(functools.partial(kernel, groups, blocks), out_shape=(jax....  49.9 us
    unnamed x4, local copies, waits for them, and re-layouts  2.74 us

profile of v3, /device:TPU:0, one launch (start us, length us, event | category | flops | bytes accessed | tf_op | source)
XLA Modules:
  0.0 55.1 jit_solution(11249581799578276924)
XLA Ops:
  0.6 49.9 %shard_map.49 = (bf16[128,2048]{1,0:T(8,128)(2,1)}, bf16[128,2048]{1,0:T(8,128)(2,1)}, f32[1,1]{1,0:T(1,128)}) custom-call(bf16[128,2048]{1,0:T(8,128)(2,1)} %view_a.1, bf16[128,2048]{1,0:T(8,128)(2,1)} %view_b.1), custom_call_target="tpu_custom_call" | custom-call | tf_op jit(solution)/shard_map/pallas_call | solution.py:317
  51.2 0.0 copy-start
  51.2 1.9 %copy.9 = bf16[128,2048]{1,0:T(8,128)(2,1)} copy(bf16[128,2048]{1,0:T(8,128)(2,1)} %get-tuple-element.13) | data formatting | bytes 1048576
  53.2 0.0 copy-done
  53.2 0.8 %copy.10 = bf16[128,2048]{1,0:T(8,128)(2,1)} copy(bf16[128,2048]{1,0:T(8,128)(2,1)S(1)} %copy-done) | data formatting | bytes 1048576
Async XLA Ops:
  51.2 2.0 %copy-start = (bf16[128,2048]{1,0:T(8,128)(2,1)S(1)}, bf16[128,2048]{1,0:T(8,128)(2,1)}, u32[]{:S(2)}) copy-start(bf16[128,2048]{1,0:T(8,128)(2,1)} %get-tuple-element.14) | copy-start | bytes 1572868

commit v4 on v3

--- a/solution.py
+++ b/solution.py
@@ -36,6 +36,7 @@
     gram,
     full,
     grads,
+    products,
     loss_core,
     loss_sample,
     loss_depth,
@@ -103,16 +104,26 @@
         own.start()
         return copies, own
 
-    lanes = [slice(k, k + BLOCK) for k in range(0, width, BLOCK)]
+    weight = OFF_WEIGHT * inv_rows
+    chunks = [slice(k, k + 64) for k in range(0, total_rows, 64)]
+
+    def octets(x):
+        return jnp.sum(x.reshape(x.shape[0] // 8, 8, x.shape[1]), axis=0)
 
     def normalize(v):
-        for cs in lanes:
-            x = raw[v, :, cs].astype(jnp.float32)
-            mean = jnp.sum(x, axis=0, keepdims=True) * inv_rows
-            square = jnp.sum(x * x, axis=0, keepdims=True) * inv_rows
-            scale = lax.rsqrt(square - mean * mean + EPSILON)
-            scales[v, :, cs] = scale
-            norm[v, :, cs] = ((x - mean) * scale).astype(jnp.bfloat16)
+        total = jnp.zeros((8, width), jnp.float32)
+        square = jnp.zeros((8, width), jnp.float32)
+        for rows in chunks:
+            x = raw[v, rows, :].astype(jnp.float32)
+            total = total + octets(x)
+            square = square + octets(x * x)
+        mean = jnp.sum(total, axis=0, keepdims=True) * inv_rows
+        square = jnp.sum(square, axis=0, keepdims=True) * inv_rows
+        scale = lax.rsqrt(square - mean * mean + EPSILON)
+        scales[v] = scale * weight
+        for rows in chunks:
+            x = raw[v, rows, :].astype(jnp.float32)
+            norm[v, rows, :] = ((x - mean) * scale).astype(jnp.bfloat16)
 
     def spot(i, j):
         first = (i * (i + 1) // 2 + j) * BLOCK
@@ -122,17 +133,24 @@
         if packed > used:
             send_core[v, used:, :] = jnp.zeros((packed - used, BLOCK), jnp.bfloat16)
             acc[v, used:, :] = jnp.zeros((packed - used, BLOCK), jnp.float32)
-        for i in range(n_blocks):
-            strip = lax.dot_general(
-                norm[v, i * BLOCK : (i + 1) * BLOCK, :],
-                norm[v, : (i + 1) * BLOCK, :],
-                (((1,), (1,)), ((), ())),
-                preferred_element_type=jnp.float32,
-            )
-            for j in range(i + 1):
-                tile = strip[:, j * BLOCK : (j + 1) * BLOCK]
-                acc[v, spot(i, j), :] = tile
-                send_core[v, spot(i, j), :] = tile.astype(jnp.bfloat16)
+        for first in range(0, n_blocks, 2):
+            last = min(first + 2, n_blocks)
+            for left in range(0, last, 2):
+                right = min(left + 2, last)
+                square = lax.dot_general(
+                    norm[v, first * BLOCK : last * BLOCK, :],
+                    norm[v, left * BLOCK : right * BLOCK, :],
+                    (((1,), (1,)), ((), ())),
+                    preferred_element_type=jnp.float32,
+                )
+                for i in range(first, last):
+                    for j in range(left, min(right, i + 1)):
+                        tile = square[
+                            (i - first) * BLOCK : (i - first + 1) * BLOCK,
+                            (j - left) * BLOCK : (j - left + 1) * BLOCK,
+                        ]
+                        acc[v, spot(i, j), :] = tile
+                        send_core[v, spot(i, j), :] = tile.astype(jnp.bfloat16)
         return [send(send_core.at[v, at(other, rows_core), :], recv_core.at[v], sibling)]
 
     def reduce_sample(v):
@@ -192,20 +210,29 @@
                     full[j * BLOCK : (j + 1) * BLOCK, i * BLOCK : (i + 1) * BLOCK] = flipped
         copies = []
         for cs in halves:
-            x = norm[v, :, cs]
-            product = lax.dot_general(
-                full[...], x, (((1,), (0,)), ((), ())), preferred_element_type=jnp.float32
+            size = cs.stop - cs.start
+            products[:, cs] = lax.dot_general(
+                full[...],
+                norm[v, :, cs],
+                (((1,), (0,)), ((), ())),
+                preferred_element_type=jnp.float32,
             )
-            x = x.astype(jnp.float32)
-            grad = (OFF_WEIGHT * inv_rows) * product + extra[:, cs] * norm[g, :, cs].astype(
-                jnp.float32
-            )
-            mean_grad = jnp.sum(grad, axis=0, keepdims=True) * inv_rows
-            mean_cross = jnp.sum(grad * x, axis=0, keepdims=True) * inv_rows
-            grads[v, :, cs] = (scales[v, :, cs] * (grad - mean_grad - x * mean_cross)).astype(
-                jnp.bfloat16
-            )
-            size = cs.stop - cs.start
+            mean_grad = jnp.zeros((8, size), jnp.float32)
+            mean_cross = jnp.zeros((8, size), jnp.float32)
+            for rows in chunks:
+                x = norm[v, rows, cs].astype(jnp.float32)
+                y = norm[g, rows, cs].astype(jnp.float32)
+                grad = products[rows, cs] + extra[:, cs] * y
+                products[rows, cs] = grad
+                mean_grad = mean_grad + octets(grad)
+                mean_cross = mean_cross + octets(grad * x)
+            mean_grad = jnp.sum(mean_grad, axis=0, keepdims=True) * inv_rows
+            mean_cross = jnp.sum(mean_cross, axis=0, keepdims=True) * inv_rows
+            scale = scales[v, :, cs]
+            for rows in chunks:
+                x = norm[v, rows, cs].astype(jnp.float32)
+                grad = products[rows, cs] - mean_grad - x * mean_cross
+                grads[v, rows, cs] = (scale * grad).astype(jnp.bfloat16)
             there = out.at[:, pl.ds(pl.multiple_of(s * width + cs.start, BLOCK), size)]
             copies += [
                 send(grads.at[v, at(peer[0], rows_dev), cs], there, peer)
@@ -238,13 +265,16 @@
     arrived(copies_b)
     normalize(1)
     step_b = reduce_core(1)
+    diag = jnp.zeros((8, width), jnp.float32)
+    for rows in chunks:
+        x = norm[0, rows, :].astype(jnp.float32) * norm[1, rows, :].astype(jnp.float32)
+        diag = diag + octets(x)
+    diag = jnp.sum(diag, axis=0, keepdims=True) * inv_rows
+    extra[...] = ((1.0 - OFF_WEIGHT) * diag - 1.0) * (1.0 / weight)
+    diag = (1.0 - diag) * (1.0 - diag) - OFF_WEIGHT * diag * diag
     part = jnp.zeros((1, BLOCK), jnp.float32)
-    for cs in lanes:
-        a = norm[0, :, cs].astype(jnp.float32)
-        b = norm[1, :, cs].astype(jnp.float32)
-        diag = jnp.sum(a * b, axis=0, keepdims=True) * inv_rows
-        extra[:, cs] = (1.0 - OFF_WEIGHT) * diag - 1.0
-        part = part + (1.0 - diag) * (1.0 - diag) - OFF_WEIGHT * diag * diag
+    for k in range(0, width, BLOCK):
+        part = part + diag[:, k : k + BLOCK]
     loss_core[c] = jnp.broadcast_to(part, (8, BLOCK))
     loss_copies = [send(loss_core.at[c], loss_core.at[c], sibling)]
 
@@ -322,7 +352,7 @@
             jax.ShapeDtypeStruct((1, 1), f32),
         ),
         in_specs=[hbm, hbm],
-        out_specs=(hbm, hbm, vmem),
+        out_specs=(vmem, vmem, vmem),
         scratch_shapes=[
             pltpu.VMEM((2, total_rows, width), bf16),
             pltpu.VMEM((2, total_rows, width), bf16),
@@ -338,6 +368,7 @@
             pltpu.VMEM((2, packed, BLOCK), bf16),
             pltpu.VMEM((total_rows, total_rows), bf16),
             pltpu.VMEM((2, total_rows, width), bf16),
+            pltpu.VMEM((total_rows, width), f32),
             pltpu.VMEM((CORES, 8, BLOCK), f32),
             pltpu.VMEM((groups, 8, BLOCK), f32),
             pltpu.VMEM((depth, 8, BLOCK), f32),
@@ -346,9 +377,12 @@
             pltpu.SemaphoreType.DMA((4,)),
         ],
         compiler_params=pltpu.CompilerParams(
-            collective_id=0, has_side_effects=True, vmem_limit_bytes=62 * 1024 * 1024
+            collective_id=0, has_side_effects=True, vmem_limit_bytes=48 * 1024 * 1024
         ),
-    )(view_a, view_b)
+    )(
+        pltpu.with_memory_space_constraint(view_a, pltpu.HBM),
+        pltpu.with_memory_space_constraint(view_b, pltpu.HBM),
+    )
     return (loss[0, 0], out_a, out_b)
 
 

time: 55.2 us -> 53.6 us (0.971)
  local copies, waits for them, and re-layouts: 2.74 us -> 1.59 us
    unnamed x4 -> x2, local copies, waits for them, and re-layouts: 2.74 us -> 1.59 us
where the time goes in v4:
time: 53.6 us; the launch traced here: 53.4 us
  Pallas kernels  49.5 us (92%)
  between operations  2.33 us (4%)
  local copies, waits for them, and re-layouts  1.59 us (3%)
    pallas_call x1, Pallas kernels, body(): pl.pallas_call(functools.partial(kernel, groups, blocks), out_shape=(jax....  49.5 us
    unnamed x2, local copies, waits for them, and re-layouts  1.59 us

profile of v4, /device:TPU:0, one launch (start us, length us, event | category | flops | bytes accessed | tf_op | source)
XLA Modules:
  0.0 53.4 jit_solution(5656692503137381393)
XLA Ops:
  0.6 49.5 %shard_map.49 = (bf16[128,2048]{1,0:T(8,128)(2,1)S(1)}, bf16[128,2048]{1,0:T(8,128)(2,1)S(1)}, f32[1,1]{1,0:T(1,128)}) custom-call(bf16[128,2048]{1,0:T(8,128)(2,1)} %view_a.1, bf16[128,2048]{1,0:T(8,128)(2,1)} %view_b.1), custom_call_target="tpu_custom_call" | custom-call | tf_op jit(solution)/shard_map/pallas_call | solution.py:347
  50.7 0.8 %copy.9 = bf16[128,2048]{1,0:T(8,128)(2,1)} copy(bf16[128,2048]{1,0:T(8,128)(2,1)S(1)} %get-tuple-element.13) | data formatting | bytes 1048576
  51.5 0.8 %copy.10 = bf16[128,2048]{1,0:T(8,128)(2,1)} copy(bf16[128,2048]{1,0:T(8,128)(2,1)S(1)} %get-tuple-element.14) | data formatting | bytes 1048576

commit v5 on v4

--- a/solution.py
+++ b/solution.py
@@ -199,7 +199,14 @@
 
     halves = [slice(k, min(k + 2 * BLOCK, width)) for k in range(0, width, 2 * BLOCK)]
 
-    def return_grad(v, out):
+    def return_half(v, out, cs):
+        first = pl.multiple_of(s * width + cs.start, BLOCK)
+        there = out.at[:, pl.ds(first, cs.stop - cs.start)]
+        return [
+            send(grads.at[v, at(peer[0], rows_dev), cs], there, peer) for peer in sample_peers
+        ]
+
+    def make_grad(v, out, finish):
         g = 1 - v
         for i in range(n_blocks):
             for j in range(i + 1):
@@ -233,11 +240,12 @@
                 x = norm[v, rows, cs].astype(jnp.float32)
                 grad = products[rows, cs] - mean_grad - x * mean_cross
                 grads[v, rows, cs] = (scale * grad).astype(jnp.bfloat16)
-            there = out.at[:, pl.ds(pl.multiple_of(s * width + cs.start, BLOCK), size)]
-            copies += [
-                send(grads.at[v, at(peer[0], rows_dev), cs], there, peer)
-                for peer in sample_peers
-            ]
+            if finish is None:
+                copies += return_half(v, out, cs)
+        if finish is not None:
+            finish()
+            for cs in halves:
+                copies += return_half(v, out, cs)
         own = pltpu.make_async_copy(
             grads.at[v, at(s, rows_dev), :], out.at[:, at(s, width)], local_sem.at[2 + v]
         )
@@ -260,6 +268,8 @@
     step_a = reduce_core(0)
     arrived(step_a)
     step_a = reduce_sample(0)
+    arrived(step_a)
+    step_a = reduce_depth(0)
 
     own_b.wait()
     arrived(copies_b)
@@ -281,19 +291,17 @@
     arrived(step_b)
     step_b = reduce_sample(1)
     arrived(step_a)
-    step_a = reduce_depth(0)
+    step_a = gather_depth(0)
     arrived(loss_copies)
     loss_sample[s] = fold(loss_core)
     loss_copies = [send(loss_sample.at[s], loss_sample.at[s], peer) for peer in sample_peers]
-    arrived(step_a)
-    step_a = gather_depth(0)
     arrived(step_b)
     step_b = reduce_depth(1)
+    arrived(step_a)
+    step_a = gather_sample(0)
     arrived(loss_copies)
     loss_depth[z] = fold(loss_sample)
     loss_copies = [send(loss_depth.at[z], loss_depth.at[z], peer) for peer in depth_peers]
-    arrived(step_a)
-    step_a = gather_sample(0)
     arrived(step_b)
     step_b = gather_depth(1)
     arrived(step_a)
@@ -301,11 +309,15 @@
     arrived(step_b)
     step_b = gather_sample(1)
     arrived(step_a)
-    returning = [return_grad(1, out_b)]
-    arrived(step_b)
-    step_b = gather_core(1)
-    arrived(step_b)
-    returning.append(return_grad(0, out_a))
+    step_a = []
+
+    def finish():
+        arrived(step_b)
+        step_a.extend(gather_core(1))
+
+    returning = [make_grad(1, out_b, finish)]
+    arrived(step_a)
+    returning.append(make_grad(0, out_a, None))
 
     arrived(loss_copies)
     product = jnp.zeros((BLOCK, BLOCK), jnp.float32)

time: 53.6 us -> 55.4 us (1.034)
  Pallas kernels: 49.5 us -> 51.4 us
    pallas_call x1, Pallas kernels: 49.5 us -> 51.4 us  [body(): pl.pallas_call(functools.partial(kernel, groups, blocks), out_shape=(jax....]
where the time goes in v5:
time: 55.4 us; the launch traced here: 55.3 us
  Pallas kernels  51.4 us (93%)
  between operations  2.33 us (4%)
  local copies, waits for them, and re-layouts  1.59 us (3%)
    pallas_call x1, Pallas kernels, body(): pl.pallas_call(functools.partial(kernel, groups, blocks), out_shape=(jax....  51.4 us
    unnamed x2, local copies, waits for them, and re-layouts  1.59 us

profile of v5, /device:TPU:0, one launch (start us, length us, event | category | flops | bytes accessed | tf_op | source)
XLA Modules:
  0.0 55.3 jit_solution(12195861098137319844)
XLA Ops:
  0.6 51.4 %shard_map.49 = (bf16[128,2048]{1,0:T(8,128)(2,1)S(1)}, bf16[128,2048]{1,0:T(8,128)(2,1)S(1)}, f32[1,1]{1,0:T(1,128)}) custom-call(bf16[128,2048]{1,0:T(8,128)(2,1)} %view_a.1, bf16[128,2048]{1,0:T(8,128)(2,1)} %view_b.1), custom_call_target="tpu_custom_call" | custom-call | tf_op jit(solution)/shard_map/pallas_call | solution.py:359
  52.6 0.8 %copy.9 = bf16[128,2048]{1,0:T(8,128)(2,1)} copy(bf16[128,2048]{1,0:T(8,128)(2,1)S(1)} %get-tuple-element.13) | data formatting | bytes 1048576
  53.4 0.8 %copy.10 = bf16[128,2048]{1,0:T(8,128)(2,1)} copy(bf16[128,2048]{1,0:T(8,128)(2,1)S(1)} %get-tuple-element.14) | data formatting | bytes 1048576

commit v6 on v4

--- a/solution.py
+++ b/solution.py
@@ -11,6 +11,7 @@
 OFF_WEIGHT = 0.0051
 BLOCK = 128
 CORES = 2
+HIGH = 2
 MESH = pl.DeviceIdType.MESH
 
 
@@ -33,6 +34,8 @@
     recv_sample,
     send_depth,
     recv_depth,
+    relay_in,
+    relay_out,
     gram,
     full,
     grads,
@@ -93,16 +96,60 @@
     def at(index, size):
         return pl.ds(pl.multiple_of(index * size, size), size)
 
+    low = groups // HIGH
+    hi, lo = lax.div(s, low), lax.rem(s, low)
+    half_rows = rows_dev // 2
+    whole, first_half, second_half = (
+        pl.ds(0, rows_dev),
+        pl.ds(0, half_rows),
+        pl.ds(half_rows, half_rows),
+    )
+
+    def there(dh, dl):
+        return lax.rem(hi + dh + HIGH, HIGH) * low + lax.rem(lo + dl + low, low)
+
+    def exchange(source, target, relay):
+        first_hop = []
+        for dh in range(1, HIGH):
+            for dl in range(1, low):
+                k = (dh - 1) * (low - 1) + dl - 1
+                to = there(dh, dl)
+                for way, rows, via in (
+                    (0, first_half, there(0, dl)),
+                    (1, second_half, there(dh, 0)),
+                ):
+                    copy = send(source(to, rows), relay.at[way, k], (via, f))
+                    first_hop.append((copy, way, k, dh, dl))
+        direct = [(0, dl) for dl in range(1, low)] + [(dh, 0) for dh in range(1, HIGH)]
+        copies = [
+            send(source(there(*d), whole), target(s, whole), (there(*d), f)) for d in direct
+        ]
+
+        def forward():
+            for copy, way, k, dh, dl in first_hop:
+                copy.wait_recv()
+                if way == 0:
+                    origin, rows, to = there(0, -dl), first_half, there(dh, 0)
+                else:
+                    origin, rows, to = there(-dh, 0), second_half, there(0, dl)
+                copies.append(send(relay.at[way, k], target(origin, rows), (to, f)))
+
+        return copies, forward
+
     def send_view(v, view):
-        copies = [
-            send(view.at[:, at(peer[0], width)], raw.at[v, at(s, rows_dev), :], peer)
-            for peer in sample_peers
-        ]
+        def source(p, rows):
+            return view.at[rows, at(p, width)]
+
+        def target(p, rows):
+            first = pl.multiple_of(p * rows_dev + rows.start, half_rows)
+            return raw.at[v, pl.ds(first, rows.size), :]
+
+        copies = exchange(source, target, relay_in.at[v])
         own = pltpu.make_async_copy(
             view.at[:, at(s, width)], raw.at[v, at(s, rows_dev), :], local_sem.at[v]
         )
         own.start()
-        return copies, own
+        return copies[0], copies[1], own
 
     weight = OFF_WEIGHT * inv_rows
     chunks = [slice(k, k + 64) for k in range(0, total_rows, 64)]
@@ -208,7 +255,6 @@
                 if j < i:
                     flipped = tile.astype(jnp.float32).T.astype(jnp.bfloat16)
                     full[j * BLOCK : (j + 1) * BLOCK, i * BLOCK : (i + 1) * BLOCK] = flipped
-        copies = []
         for cs in halves:
             size = cs.stop - cs.start
             products[:, cs] = lax.dot_general(
@@ -233,16 +279,20 @@
                 x = norm[v, rows, cs].astype(jnp.float32)
                 grad = products[rows, cs] - mean_grad - x * mean_cross
                 grads[v, rows, cs] = (scale * grad).astype(jnp.bfloat16)
-            there = out.at[:, pl.ds(pl.multiple_of(s * width + cs.start, BLOCK), size)]
-            copies += [
-                send(grads.at[v, at(peer[0], rows_dev), cs], there, peer)
-                for peer in sample_peers
-            ]
+
+        def source(p, rows):
+            first = pl.multiple_of(p * rows_dev + rows.start, half_rows)
+            return grads.at[v, pl.ds(first, rows.size), :]
+
+        def target(p, rows):
+            return out.at[rows, at(p, width)]
+
+        copies, forward = exchange(source, target, relay_out.at[v])
         own = pltpu.make_async_copy(
             grads.at[v, at(s, rows_dev), :], out.at[:, at(s, width)], local_sem.at[2 + v]
         )
         own.start()
-        return copies, own
+        return copies, forward, own
 
     def fold(slots):
         total = slots[0]
@@ -250,14 +300,14 @@
             total = total + slots[k]
         return total
 
-    copies_a, own_a = send_view(0, view_a)
-    for copy in copies_a:
-        copy.wait_send()
-    copies_b, own_b = send_view(1, view_b)
+    copies_a, forward_a, own_a = send_view(0, view_a)
+    forward_a()
+    copies_b, forward_b, own_b = send_view(1, view_b)
     own_a.wait()
     arrived(copies_a)
     normalize(0)
     step_a = reduce_core(0)
+    forward_b()
     arrived(step_a)
     step_a = reduce_sample(0)
 
@@ -304,8 +354,10 @@
     returning = [return_grad(1, out_b)]
     arrived(step_b)
     step_b = gather_core(1)
+    returning[0][1]()
     arrived(step_b)
     returning.append(return_grad(0, out_a))
+    returning[1][1]()
 
     arrived(loss_copies)
     product = jnp.zeros((BLOCK, BLOCK), jnp.float32)
@@ -319,10 +371,10 @@
     lane_loss = (fold(loss_depth)[0:1, :] + trace) * (1.0 / (cols_dev * blocks))
     loss_out[...] = jnp.sum(lane_loss, axis=1, keepdims=True)
 
-    for copies, own in returning:
+    for copies, _, own in returning:
         own.wait()
         arrived(copies)
-    for copy in started[len(copies_a) :]:
+    for copy in started:
         copy.wait_send()
 
 
@@ -339,8 +391,11 @@
     rows_core = packed // CORES
     rows_sample = rows_core // groups
     rows_depth = rows_sample // depth
-    halves = -(-width // (2 * BLOCK))
-    copies = (2 + 2 + 1 + 2 + 2 * halves) * (groups - 1) + 5 * (depth - 1) + 5
+    low = groups // HIGH
+    pairs = (HIGH - 1) * (low - 1)
+    relay = (2, 2, pairs, rows_dev // 2, width)
+    exchanged = 4 * pairs + low - 1 + HIGH - 1
+    copies = 4 * exchanged + 3 * (groups - 1) + 2 * (groups - 1) + 5 * (depth - 1) + 5
     bf16, f32 = jnp.bfloat16, jnp.float32
     vmem = pl.BlockSpec(memory_space=pltpu.VMEM)
     hbm = pl.BlockSpec(memory_space=pltpu.HBM)
@@ -365,6 +420,8 @@
             pltpu.VMEM((2, groups - 1, rows_sample, BLOCK), bf16),
             pltpu.VMEM((2, rows_sample, BLOCK), bf16),
             pltpu.VMEM((2, depth - 1, rows_depth, BLOCK), bf16),
+            pltpu.VMEM(relay, bf16),
+            pltpu.VMEM(relay, bf16),
             pltpu.VMEM((2, packed, BLOCK), bf16),
             pltpu.VMEM((total_rows, total_rows), bf16),
             pltpu.VMEM((2, total_rows, width), bf16),

time: 53.6 us -> 53.6 us (level)
  no operation moved by 1% of the time
where the time goes in v6:
time: 53.6 us; the launch traced here: 53.4 us
  Pallas kernels  49.5 us (92%)
  between operations  2.33 us (4%)
  local copies, waits for them, and re-layouts  1.59 us (3%)
    pallas_call x1, Pallas kernels, body(): pl.pallas_call(functools.partial(kernel, groups, blocks), out_shape=(jax....  49.5 us
    unnamed x2, local copies, waits for them, and re-layouts  1.59 us

profile of v6, /device:TPU:0, one launch (start us, length us, event | category | flops | bytes accessed | tf_op | source)
XLA Modules:
  0.0 53.4 jit_solution(357828816191872227)
XLA Ops:
  0.6 49.5 %shard_map.49 = (bf16[128,2048]{1,0:T(8,128)(2,1)S(1)}, bf16[128,2048]{1,0:T(8,128)(2,1)S(1)}, f32[1,1]{1,0:T(1,128)}) custom-call(bf16[128,2048]{1,0:T(8,128)(2,1)} %view_a.1, bf16[128,2048]{1,0:T(8,128)(2,1)} %view_b.1), custom_call_target="tpu_custom_call" | custom-call | tf_op jit(solution)/shard_map/pallas_call | solution.py:402
  50.7 0.8 %copy.9 = bf16[128,2048]{1,0:T(8,128)(2,1)} copy(bf16[128,2048]{1,0:T(8,128)(2,1)S(1)} %get-tuple-element.13) | data formatting | bytes 1048576
  51.5 0.8 %copy.10 = bf16[128,2048]{1,0:T(8,128)(2,1)} copy(bf16[128,2048]{1,0:T(8,128)(2,1)S(1)} %get-tuple-element.14) | data formatting | bytes 1048576

commit v7 on v4

--- a/solution.py
+++ b/solution.py
@@ -29,10 +29,10 @@
     acc,
     send_core,
     recv_core,
-    send_sample,
-    recv_sample,
-    send_depth,
-    recv_depth,
+    send_first,
+    recv_first,
+    send_second,
+    recv_second,
     gram,
     full,
     grads,
@@ -53,8 +53,7 @@
     used = n_blocks * (n_blocks + 1) // 2 * BLOCK
     packed = acc.shape[1]
     rows_core = packed // CORES
-    rows_sample = rows_core // groups
-    rows_depth = rows_sample // depth
+    rows_last = rows_core // (groups * depth)
     s = lax.axis_index("sample")
     f = lax.axis_index("feat")
     z = lax.div(f, CORES)
@@ -153,46 +152,58 @@
                         send_core[v, spot(i, j), :] = tile.astype(jnp.bfloat16)
         return [send(send_core.at[v, at(other, rows_core), :], recv_core.at[v], sibling)]
 
-    def reduce_sample(v):
+    def position(peer):
+        return lax.div(peer[1], CORES)
+
+    along = (
+        (depth_peers, position, z, depth),
+        (sample_peers, lambda peer: peer[0], s, groups),
+    )
+
+    def reduce_first(v):
+        receivers, index, _, count = along[v]
+        rows = rows_core // count
         mine = at(c, rows_core)
         total = acc[v, mine, :] + recv_core[v].astype(jnp.float32)
         acc[v, mine, :] = total
-        send_sample[v] = total.astype(jnp.bfloat16)
+        send_first[v] = total.astype(jnp.bfloat16)
         return [
-            send(send_sample.at[v, at(peer[0], rows_sample), :], recv_sample.at[v, k], peer)
-            for k, peer in enumerate(sample_peers)
+            send(send_first.at[v, at(index(peer), rows), :], recv_first.at[v, k, :rows], peer)
+            for k, peer in enumerate(receivers)
         ]
 
-    def reduce_depth(v):
-        mine = at(c * groups + s, rows_sample)
+    def reduce_second(v):
+        _, _, me, count = along[v]
+        receivers, index, _, _ = along[1 - v]
+        rows = rows_core // count
+        mine = at(c * count + me, rows)
         total = acc[v, mine, :]
-        for k in range(groups - 1):
-            total = total + recv_sample[v, k].astype(jnp.float32)
+        for k in range(count - 1):
+            total = total + recv_first[v, k, :rows].astype(jnp.float32)
         acc[v, mine, :] = total
-        send_depth[v] = total.astype(jnp.bfloat16)
+        send_second[v, :rows] = total.astype(jnp.bfloat16)
         return [
-            send(
-                send_depth.at[v, at(lax.div(peer[1], CORES), rows_depth), :],
-                recv_depth.at[v, k],
-                peer,
-            )
-            for k, peer in enumerate(depth_peers)
+            send(send_second.at[v, at(index(peer), rows_last), :], recv_second.at[v, k], peer)
+            for k, peer in enumerate(receivers)
         ]
 
     def spread(v, rows, receivers):
         here = gram.at[v, rows, :]
         return [send(here, here, peer) for peer in receivers]
 
-    def gather_depth(v):
-        mine = at((c * groups + s) * depth + z, rows_depth)
+    def gather_second(v):
+        _, _, me, count = along[v]
+        receivers, _, inner, inner_count = along[1 - v]
+        mine = at((c * count + me) * inner_count + inner, rows_last)
         total = acc[v, mine, :]
-        for k in range(depth - 1):
-            total = total + recv_depth[v, k].astype(jnp.float32)
+        for k in range(inner_count - 1):
+            total = total + recv_second[v, k].astype(jnp.float32)
         gram[v, mine, :] = total.astype(jnp.bfloat16)
-        return spread(v, mine, depth_peers)
-
-    def gather_sample(v):
-        return spread(v, at(c * groups + s, rows_sample), sample_peers)
+        return spread(v, mine, receivers)
+
+    def gather_first(v):
+        receivers, _, me, count = along[v]
+        return spread(v, at(c * count + me, rows_core // count), receivers)
 
     def gather_core(v):
         return spread(v, at(c, rows_core), [sibling])
@@ -259,7 +270,7 @@
     normalize(0)
     step_a = reduce_core(0)
     arrived(step_a)
-    step_a = reduce_sample(0)
+    step_a = reduce_first(0)
 
     own_b.wait()
     arrived(copies_b)
@@ -279,27 +290,27 @@
     loss_copies = [send(loss_core.at[c], loss_core.at[c], sibling)]
 
     arrived(step_b)
-    step_b = reduce_sample(1)
-    arrived(step_a)
-    step_a = reduce_depth(0)
+    step_b = reduce_first(1)
+    arrived(step_a)
+    step_a = reduce_second(0)
     arrived(loss_copies)
     loss_sample[s] = fold(loss_core)
     loss_copies = [send(loss_sample.at[s], loss_sample.at[s], peer) for peer in sample_peers]
     arrived(step_a)
-    step_a = gather_depth(0)
-    arrived(step_b)
-    step_b = reduce_depth(1)
+    step_a = gather_second(0)
+    arrived(step_b)
+    step_b = reduce_second(1)
     arrived(loss_copies)
     loss_depth[z] = fold(loss_sample)
     loss_copies = [send(loss_depth.at[z], loss_depth.at[z], peer) for peer in depth_peers]
     arrived(step_a)
-    step_a = gather_sample(0)
-    arrived(step_b)
-    step_b = gather_depth(1)
+    step_a = gather_first(0)
+    arrived(step_b)
+    step_b = gather_second(1)
     arrived(step_a)
     step_a = gather_core(0)
     arrived(step_b)
-    step_b = gather_sample(1)
+    step_b = gather_first(1)
     arrived(step_a)
     returning = [return_grad(1, out_b)]
     arrived(step_b)
@@ -337,8 +348,8 @@
     step = CORES * groups * depth * 16
     packed = -(-(n_blocks * (n_blocks + 1) // 2 * BLOCK) // step) * step
     rows_core = packed // CORES
-    rows_sample = rows_core // groups
-    rows_depth = rows_sample // depth
+    rows_last = rows_core // (groups * depth)
+    most, least = max(groups, depth), min(groups, depth)
     halves = -(-width // (2 * BLOCK))
     copies = (2 + 2 + 1 + 2 + 2 * halves) * (groups - 1) + 5 * (depth - 1) + 5
     bf16, f32 = jnp.bfloat16, jnp.float32
@@ -362,9 +373,9 @@
             pltpu.VMEM((2, packed, BLOCK), bf16),
             pltpu.VMEM((2, rows_core, BLOCK), bf16),
             pltpu.VMEM((2, rows_core, BLOCK), bf16),
-            pltpu.VMEM((2, groups - 1, rows_sample, BLOCK), bf16),
-            pltpu.VMEM((2, rows_sample, BLOCK), bf16),
-            pltpu.VMEM((2, depth - 1, rows_depth, BLOCK), bf16),
+            pltpu.VMEM((2, most - 1, rows_core // least, BLOCK), bf16),
+            pltpu.VMEM((2, rows_core // least, BLOCK), bf16),
+            pltpu.VMEM((2, most - 1, rows_last, BLOCK), bf16),
             pltpu.VMEM((2, packed, BLOCK), bf16),
             pltpu.VMEM((total_rows, total_rows), bf16),
             pltpu.VMEM((2, total_rows, width), bf16),

time: 53.6 us -> 55.6 us (1.037)
  Pallas kernels: 49.5 us -> 51.5 us
    pallas_call x1, Pallas kernels: 49.5 us -> 51.5 us  [body(): pl.pallas_call(functools.partial(kernel, groups, blocks), out_shape=(jax....]
where the time goes in v7:
time: 55.6 us; the launch traced here: 55.4 us
  Pallas kernels  51.5 us (93%)
  between operations  2.33 us (4%)
  local copies, waits for them, and re-layouts  1.59 us (3%)
    pallas_call x1, Pallas kernels, body(): pl.pallas_call(functools.partial(kernel, groups, blocks), out_shape=(jax....  51.5 us
    unnamed x2, local copies, waits for them, and re-layouts  1.59 us

profile of v7, /device:TPU:0, one launch (start us, length us, event | category | flops | bytes accessed | tf_op | source)
XLA Modules:
  0.0 55.4 jit_solution(17382944566204479737)
XLA Ops:
  0.6 51.5 %shard_map.49 = (bf16[128,2048]{1,0:T(8,128)(2,1)S(1)}, bf16[128,2048]{1,0:T(8,128)(2,1)S(1)}, f32[1,1]{1,0:T(1,128)}) custom-call(bf16[128,2048]{1,0:T(8,128)(2,1)} %view_a.1, bf16[128,2048]{1,0:T(8,128)(2,1)} %view_b.1), custom_call_target="tpu_custom_call" | custom-call | tf_op jit(solution)/shard_map/pallas_call | solution.py:358
  52.7 0.8 %copy.9 = bf16[128,2048]{1,0:T(8,128)(2,1)} copy(bf16[128,2048]{1,0:T(8,128)(2,1)S(1)} %get-tuple-element.13) | data formatting | bytes 1048576
  53.5 0.8 %copy.10 = bf16[128,2048]{1,0:T(8,128)(2,1)} copy(bf16[128,2048]{1,0:T(8,128)(2,1)S(1)} %get-tuple-element.14) | data formatting | bytes 1048576
